TPU v7x, 256 devices: a whole 4x4x8 slice. The times are simulated.
256 devices in a mesh: rows: 8 (over z), hidden: 32 (over x, y, core).
Axes of the slice: x: 4, y: 4, z: 8, core: 2. Of those that a mesh axis runs over, the one named last changes fastest.
Arguments:
- tokens: bfloat16 [1024, 8192], P('hidden', 'rows'), may hold values from -6 to 6
- snapshot: int32 [1024, 1], replicated, may hold values from 0 to 63; in each aligned block of 1024 rows (0 to 1023, 1024 to 2047, ...) at most 32 rows name the same one
- gate_weight: bfloat16 [8192, 28672], P('rows', 'hidden'), may hold values from -0.0625 to 0.0625
- up_weight: bfloat16 [8192, 28672], P('rows', 'hidden'), may hold values from -0.0625 to 0.0625
- down_weight: bfloat16 [28672, 8192], P('hidden', 'rows'), may hold values from -0.03125 to 0.03125
- adapter_input_maps: bfloat16 [64, 8192, 128], P('hidden', 'rows')
- adapter_middle_maps: bfloat16 [64, 2, 64, 28672], P(None, None, 'rows', 'hidden'), may hold values from -0.375 to 0.375
- down_input_map: bfloat16 [64, 64, 28672], P(None, 'rows', 'hidden')
- down_output_map: bfloat16 [64, 64, 8192], P('hidden', None, 'rows'), may hold values from -0.75 to 0.75
Outputs:
- mixed: bfloat16 [1024, 8192], P('hidden', 'rows')
Inputs may be any that keep to these rules, and one draw needn't show every extreme that they name: Every snapshot is named by at least one row and by at most 32 rows; some snapshot is named by exactly 32 rows.
All inputs are finite; a program needn't handle non-finite values.
Results may differ from a plain program's by a relative error of at most 0.033.
Values may be sent and summed in bfloat16 or wider, within the bound.
No kernel may reach another device: no remote copies, remote signals or barrier semaphores. Data moves between devices by JAX's collectives and lax.ppermute only.
A program may use at most 128 MiB of HBM per device.

v0:
```python
import jax
import jax.numpy as jnp
from jax import lax
from jax.sharding import PartitionSpec as P


def slot_tables(snapshot, snapshot_total, capacity):
    row_total = snapshot.shape[0]
    snap_owner = snapshot[:, 0]
    onehot = (snap_owner[:, None] == jnp.arange(snapshot_total, dtype=jnp.int32)[None, :]).astype(
        jnp.int32
    )
    before = jnp.cumsum(onehot, axis=0) - onehot
    slot_index = jnp.sum(before * onehot, axis=1)
    token_of = jnp.full((snapshot_total, capacity), row_total, jnp.int32)
    token_of = token_of.at[snap_owner, slot_index].set(jnp.arange(row_total, dtype=jnp.int32))
    return (snap_owner, slot_index, token_of)


def swiglu(paired):
    return (jax.nn.silu(paired[:, 0]) * paired[:, 1]).astype(jnp.bfloat16)


def per_device(
    tokens,
    snapshot,
    gate_weight,
    up_weight,
    down_weight,
    adapter_input_maps,
    adapter_middle_maps,
    down_input_map,
    down_output_map,
):
    row_index = lax.axis_index("rows")
    hidden_index = lax.axis_index("hidden")
    all_count = snapshot.shape[0]
    snapshot_total = adapter_middle_maps.shape[0]
    capacity = 2 * all_count // snapshot_total
    snapshot_local = adapter_input_maps.shape[0]
    rank_block_values = adapter_middle_maps.shape[2]
    rank_full = down_output_map.shape[1]
    snap_owner, slot_index, token_of = slot_tables(snapshot, snapshot_total, capacity)
    filled_flag = token_of < all_count
    clamped_index = jnp.minimum(token_of, all_count - 1)
    own_first = hidden_index * snapshot_local
    own_clamped = lax.dynamic_slice_in_dim(clamped_index, own_first, snapshot_local, 0)
    own_filled = lax.dynamic_slice_in_dim(filled_flag, own_first, snapshot_local, 0)
    own_tokens = lax.dynamic_slice_in_dim(token_of, own_first, snapshot_local, 0)
    gathered = lax.all_gather(tokens, "hidden", axis=0, tiled=True)
    picked_snapshot = jnp.where(
        own_filled[:, :, None], gathered[own_clamped], jnp.zeros((), gathered.dtype)
    )
    rank_partial_values = jnp.einsum(
        "leh,lhr->ler", picked_snapshot, adapter_input_maps, preferred_element_type=jnp.float32
    )
    rank_partial_values = rank_partial_values.reshape(snapshot_local, capacity, 2, rank_full)
    placed = jnp.zeros((snapshot_total, capacity, 2, rank_full), jnp.float32)
    placed = lax.dynamic_update_slice_in_dim(placed, rank_partial_values, own_first, 0)
    rank_total = lax.psum(placed, ("rows", "hidden"))
    rank_activation_values = lax.dynamic_slice_in_dim(
        rank_total, row_index * rank_block_values, rank_block_values, 3
    ).astype(jnp.bfloat16)
    halves = []
    for half_position in range(2):
        grouped_rows = jnp.einsum(
            "sck,skf->scf",
            rank_activation_values[:, :, half_position],
            adapter_middle_maps[:, half_position],
            preferred_element_type=jnp.float32,
        )
        halves.append(grouped_rows[snap_owner, slot_index])
    adapter_gate_up = jnp.stack(halves, axis=1)
    gate_term = jnp.dot(gathered, gate_weight, preferred_element_type=jnp.float32)
    up_term = jnp.dot(gathered, up_weight, preferred_element_type=jnp.float32)
    adapter_rows = adapter_gate_up
    summed = lax.psum(
        (jnp.stack([gate_term, up_term], axis=1) + adapter_rows).astype(jnp.bfloat16), "rows"
    ).astype(jnp.float32)
    hidden_all = swiglu(summed)
    rows_grouped = jnp.where(
        filled_flag[:, :, None], hidden_all[clamped_index], jnp.zeros((), hidden_all.dtype)
    )
    down_part = jnp.einsum(
        "scf,skf->sck", rows_grouped, down_input_map, preferred_element_type=jnp.float32
    )
    placed_down = jnp.zeros((snapshot_total, capacity, rank_full), jnp.float32)
    placed_down = lax.dynamic_update_slice_in_dim(
        placed_down, down_part, row_index * rank_block_values, 2
    )
    down_total = lax.psum(placed_down, ("rows", "hidden"))
    down_rank = lax.dynamic_slice_in_dim(down_total, own_first, snapshot_local, 0).astype(
        jnp.bfloat16
    )
    lifted = jnp.einsum(
        "sck,skd->scd", down_rank, down_output_map, preferred_element_type=jnp.float32
    )
    feature_width = lifted.shape[2]
    adapter_down = jnp.zeros((all_count + 1, feature_width), jnp.float32)
    adapter_down = adapter_down.at[own_tokens.reshape(-1)].add(lifted.reshape(-1, feature_width))[
        :all_count
    ]
    adapter_rows = adapter_down
    return lax.psum_scatter(
        (
            jnp.dot(hidden_all, down_weight, preferred_element_type=jnp.float32) + adapter_rows
        ).astype(jnp.bfloat16),
        "hidden",
        scatter_dimension=0,
        tiled=True,
    )


def solution(mesh):
    return jax.shard_map(
        per_device,
        mesh=mesh,
        in_specs=(
            P("hidden", "rows"),
            P(),
            P("rows", "hidden"),
            P("rows", "hidden"),
            P("hidden", "rows"),
            P("hidden", "rows", None),
            P(None, None, "rows", "hidden"),
            P(None, "rows", "hidden"),
            P("hidden", None, "rows"),
        ),
        out_specs=P("hidden", "rows"),
        check_vma=False,
    )
```

profile of v0, /device:TPU:2, one launch (start us, length us, event | category | flops | bytes accessed | tf_op | source)
XLA Modules:
  0.0 571.1 jit_solution(12695949925899009694)
XLA Ops:
  6.5 0.0 copy-start
  6.5 0.0 all-gather.2.cloned.1.call-start
  6.5 0.7 all-gather.2.cloned.1.call-update
  7.3 0.0 all-reduce.4.cloned.1.call-start
  7.3 0.7 fusion.19
  8.0 18.0 %reduce-window.6 = s32[64,8,128]{2,1,0:T(8,128)S(1)} reduce-window(s32[64,8,128]{2,1,0:T(8,128)S(1)} %fusion.19, s32[]{:T(128)} %constant.16.clone.1), window={size=1x1x128 pad=0_0x0_0x127_0}, to_apply=%region_0.0 | reduce-window | flops 8323072 | bytes 524292 | tf_op jit(solution)/shard_map/reduce-window
  26.0 0.1 slice.44
  26.2 0.1 copy.13
  26.4 0.1 copy.14
  26.4 0.1 broadcast_add_fusion
  26.6 0.8 fusion.18
  27.3 0.7 shift-left_or_fusion
  28.1 0.7 multiply_reduce_fusion
  28.8 0.8 and_reduce_fusion
  29.6 4.3 scatter_custom_fusion.1
  33.9 0.1 reshape.74
  34.0 0.1 compare_select_fusion.1
  34.1 0.1 copy.16
  34.1 0.1 reshape.78
  34.2 0.1 dynamic-slice_bitcast_fusion.1
  34.3 0.1 copy.15
  34.4 26.9 %all-gather.2.cloned.1.call-done = bf16[1024,1024]{1,0:T(8,128)(2,1)} async-done(((bf16[32,1024]{1,0:T(8,128)(2,1)}), bf16[1024,1024]{1,0:T(8,128)(2,1)}) %all-gather.2.cloned.1.call-update) | async-done | bytes 2097168 | tf_op jit(solution)/shard_map/all_gather | solution.py:50
  61.4 2.7 gather_fusion
  64.0 0.0 copy-done.5
  64.0 0.3 fusion.20
  64.3 0.1 reshape.69
  64.4 0.1 copy.17
  64.5 2.5 broadcast_in_dim.49
  67.0 0.6 constant_dynamic-update-slice_fusion
  67.6 130.6 %all-reduce.5 = bf16[64,32,2,64]{1,3,0,2:T(8,128)(2,1)} all-reduce(f32[64,32,2,64]{1,3,0,2:T(8,128)} %constant_dynamic-update-slice_fusion), channel_id=1, replica_groups=mesh['rows'=8,'hidden'=32] {'rows','hidden'}, use_global_device_ids=true, to_apply=%region_4.5 | all-reduce | flops 262144 | bytes 1572864 | tf_op jit(solution)/shard_map/psum | solution.py:60
  198.2 1.0 dynamic-slice_convert_fusion
  199.2 0.0 copy-start.3
  199.2 5.5 fusion.12
  204.7 0.0 copy-done.3
  204.7 4.1 fusion.10
  208.8 19.8 %gather_fusion.1 = f32[1024,896]{1,0:T(8,128)} fusion(f32[64,32,896]{2,1,0:T(8,128)} %fusion.12, s32[1024]{0:T(1024)S(1)} %bitcast.78), kind=kCustom, calls=%fused_computation.1 | custom fusion | bytes 7348224 | tf_op jit(solution)/shard_map/gather | solution.py:72
  228.7 19.9 %gather_fusion.2 = f32[1024,896]{1,0:T(8,128)} fusion(f32[64,32,896]{2,1,0:T(8,128)} %fusion.10, s32[1024]{0:T(1024)S(1)} %bitcast.79), kind=kCustom, calls=%fused_computation.2 | custom fusion | bytes 7348224 | tf_op jit(solution)/shard_map/gather | solution.py:72
  248.5 4.6 convolution_bitcast_fusion
  253.2 0.0 copy-done.4
  253.2 2.3 convolution_bitcast_fusion.1
  255.5 0.0 copy-done.1
  255.5 0.8 copy-done.2
  256.3 2.1 fusion
  258.5 0.0 all-reduce.4.cloned.1.call-update
  258.5 0.2 reduce-scatter.2.cloned.1.call-start
  258.7 0.1 copy.22
  258.8 0.1 reshape.98
  258.9 0.1 copy.21
  259.0 0.1 dynamic-slice_bitcast_fusion
  259.1 0.1 copy.20
  259.2 0.1 reshape.70
  259.3 96.2 %all-reduce.4.cloned.1.call-done = bf16[1024,2,896]{2,0,1:T(8,128)(2,1)} async-done(((bf16[1024,2,896]{2,0,1:T(8,128)(2,1)}), bf16[1024,2,896]{2,0,1:T(8,128)(2,1)}) %all-reduce.4.cloned.1.call-update) | async-done | bytes 3670032 | tf_op jit(solution)/shard_map/psum | solution.py:77
  355.5 2.5 convert_element_type.29
  358.0 2.3 fusion.3
  360.3 12.3 %gather_fusion.3 = bf16[2048,896]{1,0:T(8,128)(2,1)} fusion(bf16[1024,896]{1,0:T(8,128)(2,1)} %fusion.3, s32[2048]{0:T(1024)S(1)} %broadcast_clamp_fusion), kind=kCustom, calls=%fused_computation.3 | custom fusion | bytes 7348224 | tf_op jit(solution)/shard_map/gather | solution.py:82
  372.6 4.2 fusion.4
  376.7 0.1 broadcast_in_dim.54
  376.9 5.2 dynamic_update_slice.7
  382.0 86.1 %all-reduce.6 = bf16[64,32,64]{2,1,0:T(8,128)(2,1)S(1)} all-reduce(f32[64,32,64]{2,1,0:T(8,128)S(1)} %dynamic_update_slice.7), channel_id=1, replica_groups=mesh['rows'=8,'hidden'=32] {'rows','hidden'}, use_global_device_ids=true, to_apply=%region_6.7 | all-reduce | flops 131072 | bytes 786432 | tf_op jit(solution)/shard_map/psum | solution.py:91
  468.1 1.1 fusion.24
  469.2 3.3 scatter_custom_fusion
  472.5 6.4 %fusion.1 = bf16[1024,1024]{1,0:T(8,128)(2,1)} fusion(f32[1025,1024]{1,0:T(8,128)} %scatter_custom_fusion, bf16[1024,896]{1,0:T(8,128)(2,1)} %fusion.3, bf16[896,1024]{1,0:T(8,128)(2,1)S(1)} %copy-done), kind=kOutput, calls=%fused_computation.9 | convolution fusion | flops 1881145344 | bytes 9961472 | tf_op jit(solution)/shard_map/dot_general | solution.py:106
  478.9 0.0 reduce-scatter.2.cloned.1.call-update
  478.9 85.7 %reduce-scatter.2.cloned.1.call-done = bf16[32,1024]{1,0:T(8,128)(2,1)} async-done(((bf16[1024,1024]{1,0:T(8,128)(2,1)}), bf16[32,1024]{1,0:T(8,128)(2,1)}) %reduce-scatter.2.cloned.1.call-update) | async-done | bytes 65552 | tf_op jit(solution)/shard_map/reduce_scatter | solution.py:104
  (20 shorter events, 0.1 us)
Async XLA Ops:
  6.5 466.0 %copy-start = (bf16[896,1024]{1,0:T(8,128)(2,1)S(1)}, bf16[896,1024]{1,0:T(8,128)(2,1)}, u32[]{:S(2)}) copy-start(bf16[896,1024]{1,0:T(8,128)(2,1)} %param.13) | copy-start | bytes 5505028
  6.5 57.5 %copy-start.5 = (bf16[2,1024,128]{2,1,0:T(8,128)(2,1)S(1)}, bf16[2,1024,128]{2,1,0:T(8,128)(2,1)}, u32[]{:S(2)}) copy-start(bf16[2,1024,128]{2,1,0:T(8,128)(2,1)} %param.14) | copy-start | bytes 1572868
  6.5 54.8 %all-gather.2.cloned.1.call-start = ((), (), s32[]{:S(2)}) async-start(), calls=%async_computation.1 | async-start | bytes 2162688 | tf_op jit(solution)/shard_map/all_gather | solution.py:50
  7.3 348.2 %all-reduce.4.cloned.1.call-start = ((), (), s32[]{:S(2)}) async-start(), calls=%async_computation.2 | async-start | bytes 7340032 | tf_op jit(solution)/shard_map/psum | solution.py:77
  199.2 5.5 copy-start.3
  248.5 4.6 copy-start.4
  248.5 4.6 copy-start.6
  253.2 2.3 copy-start.1
  253.2 3.2 copy-start.2
  258.5 306.1 %reduce-scatter.2.cloned.1.call-start = ((), (), s32[]{:S(2)}) async-start(), calls=%async_computation.3 | async-start | bytes 2162688 | tf_op jit(solution)/shard_map/reduce_scatter | solution.py:104
  360.3 12.3 %copy-start.7 = (bf16[64,8,896]{2,1,0:T(8,128)(2,1)S(1)}, bf16[64,8,896]{2,1,0:T(8,128)(2,1)}, u32[]{:S(2)}) copy-start(bf16[64,8,896]{2,1,0:T(8,128)(2,1)} %param.16) | copy-start | bytes 2752516
Sparse Core Ops, SparseCore 0:
  9.9 51.3 all-gather.1
  258.6 96.7 all-reduce.3
  479.0 85.4 reduce-scatter.1
where the time goes:
time: 572 us; the launch traced here: 571 us
  blocking collectives  217 us (38%)
  waiting for transfers between devices  210 us (37%)
  local copies, waits for them, and re-layouts  70.6 us (12%)
  other arithmetic  32.2 us (6%)
  matrix products  28.5 us (5%)
  between operations  13.3 us (2%)
    psum x1, blocking collectives, per_device(): rank_total = lax.psum(placed, ('rows', 'hidden'))  131 us
    psum x1, waiting for transfers between devices, per_device(): lax.psum((jnp.stack([gate_term, up_term], axis=1) + adapter_rows).astype(...  96.2 us
    psum x1, blocking collectives, per_device(): down_total = lax.psum(placed_down, ('rows', 'hidden'))  86.1 us
    reduce_scatter x1, waiting for transfers between devices, per_device(): lax.psum_scatter((jnp.dot(hidden_all, down_weight, preferred_element_type...  85.7 us
    gather x2, local copies, waits for them, and re-layouts, per_device(): halves.append(grouped_rows[snap_owner, slot_index])  39.7 us
    all_gather x1, waiting for transfers between devices, per_device(): gathered = lax.all_gather(tokens, 'hidden', axis=0, tiled=True)  26.9 us
    another operation x3, other arithmetic  18.2 us
    gather x1, local copies, waits for them, and re-layouts, per_device(): hidden_all[clamped_index]  12.3 us
  transfers between devices with their start and end apart: 3, of which 3 were waited for; matrix products, arithmetic and copies ran while one was open for 5% of the time, Pallas kernels for 0%

commit v1 on v0

--- a/solution.py
+++ b/solution.py
@@ -2,6 +2,7 @@
 import jax.numpy as jnp
 from jax import lax
 from jax.sharding import PartitionSpec as P
+from jax.lax import psum
 
 
 def slot_tables(snapshot, snapshot_total, capacity):
@@ -57,7 +58,7 @@
     rank_partial_values = rank_partial_values.reshape(snapshot_local, capacity, 2, rank_full)
     placed = jnp.zeros((snapshot_total, capacity, 2, rank_full), jnp.float32)
     placed = lax.dynamic_update_slice_in_dim(placed, rank_partial_values, own_first, 0)
-    rank_total = lax.psum(placed, ("rows", "hidden"))
+    rank_total = psum(psum(placed, "hidden"), "rows")
     rank_activation_values = lax.dynamic_slice_in_dim(
         rank_total, row_index * rank_block_values, rank_block_values, 3
     ).astype(jnp.bfloat16)

time: 572 us -> 652 us (1.14)
  waiting for transfers between devices: 210 us -> 321 us
  blocking collectives: 217 us -> 176 us
    psum x0 -> x1, waiting for transfers between devices: none -> 110 us  [per_device(): rank_total = psum(psum(placed, 'hidden'), 'rows')]
    psum x1, blocking collectives: 131 us -> 90.4 us  [per_device(): rank_total = psum(psum(placed, 'hidden'), 'rows')]
  transfers between devices with their start and end apart: 3 -> 4, of which waited for: 3 -> 4; matrix products, arithmetic and copies ran while one was open for 5% -> 6% of each run, Pallas kernels for 0% -> 0%
where the time goes in v1:
time: 652 us; the launch traced here: 650 us
  waiting for transfers between devices  321 us (49%)
  blocking collectives  176 us (27%)
  local copies, waits for them, and re-layouts  69.9 us (11%)
  other arithmetic  37.5 us (6%)
  matrix products  32.1 us (5%)
  between operations  13.3 us (2%)
    psum x1, waiting for transfers between devices, per_device(): rank_total = psum(psum(placed, 'hidden'), 'rows')  110 us
    psum x1, waiting for transfers between devices, per_device(): lax.psum((jnp.stack([gate_term, up_term], axis=1) + adapter_rows).astype(...  97.2 us
    psum x1, blocking collectives, per_device(): rank_total = psum(psum(placed, 'hidden'), 'rows')  90.4 us
    psum x1, blocking collectives, per_device(): down_total = lax.psum(placed_down, ('rows', 'hidden'))  86.1 us
    reduce_scatter x1, waiting for transfers between devices, per_device(): lax.psum_scatter((jnp.dot(hidden_all, down_weight, preferred_element_type...  85.7 us
    gather x2, local copies, waits for them, and re-layouts, per_device(): halves.append(grouped_rows[snap_owner, slot_index])  39.7 us
    all_gather x1, waiting for transfers between devices, per_device(): gathered = lax.all_gather(tokens, 'hidden', axis=0, tiled=True)  26.9 us
    another operation x3, other arithmetic  18.2 us
  transfers between devices with their start and end apart: 4, of which 4 were waited for; matrix products, arithmetic and copies ran while one was open for 6% of the time, Pallas kernels for 0%

profile of v1, /device:TPU:2, one launch (start us, length us, event | category | flops | bytes accessed | tf_op | source)
XLA Modules:
  0.0 650.5 jit_solution(17582307295862246170)
XLA Ops:
  6.5 0.0 copy-start
  6.5 0.0 all-gather.2.cloned.1.call-start
  6.5 0.7 all-gather.2.cloned.1.call-update
  7.3 0.0 all-reduce.5.cloned.1.call-start
  7.3 0.7 fusion.19
  8.0 18.0 %reduce-window.6 = s32[64,8,128]{2,1,0:T(8,128)S(1)} reduce-window(s32[64,8,128]{2,1,0:T(8,128)S(1)} %fusion.19, s32[]{:T(128)} %constant.16.clone.1), window={size=1x1x128 pad=0_0x0_0x127_0}, to_apply=%region_0.0 | reduce-window | flops 8323072 | bytes 524292 | tf_op jit(solution)/shard_map/reduce-window
  26.0 0.1 slice.44
  26.2 0.1 copy.13
  26.4 0.1 copy.14
  26.4 0.1 broadcast_add_fusion
  26.6 0.8 fusion.18
  27.3 0.7 shift-left_or_fusion
  28.1 0.7 multiply_reduce_fusion
  28.8 0.8 and_reduce_fusion
  29.6 4.3 scatter_custom_fusion.1
  33.9 0.1 reshape.74
  34.0 0.1 compare_select_fusion.1
  34.1 0.1 copy.16
  34.1 0.1 reshape.78
  34.2 0.1 dynamic-slice_bitcast_fusion.1
  34.3 0.1 copy.15
  34.4 26.9 %all-gather.2.cloned.1.call-done = bf16[1024,1024]{1,0:T(8,128)(2,1)} async-done(((bf16[32,1024]{1,0:T(8,128)(2,1)}), bf16[1024,1024]{1,0:T(8,128)(2,1)}) %all-gather.2.cloned.1.call-update) | async-done | bytes 2097168 | tf_op jit(solution)/shard_map/all_gather | solution.py:51
  61.4 2.7 gather_fusion
  64.0 0.3 fusion.20
  64.3 0.1 reshape.69
  64.4 0.1 copy.17
  64.5 2.5 broadcast_in_dim.49
  67.0 0.6 constant_dynamic-update-slice_fusion
  67.7 0.0 all-reduce.5.cloned.1.call-update
  67.7 0.0 all-reduce.7.cloned.1.call-start
  67.7 0.0 copy-start.4
  67.7 6.4 convolution_bitcast_fusion
  74.1 4.2 convolution_bitcast_fusion.1
  78.3 110.3 %all-reduce.5.cloned.1.call-done = f32[64,32,2,64]{1,3,0,2:T(8,128)} async-done(((f32[64,32,2,64]{1,3,0,2:T(8,128)}), f32[64,32,2,64]{1,3,0,2:T(8,128)}) %all-reduce.5.cloned.1.call-update) | async-done | bytes 1048592 | tf_op jit(solution)/shard_map/psum | solution.py:61
  188.7 90.4 %all-reduce.8 = bf16[64,32,2,64]{1,3,0,2:T(8,128)(2,1)} all-reduce(f32[64,32,2,64]{1,3,0,2:T(8,128)} %all-reduce.5.cloned.1.call-done), channel_id=1, replica_groups=mesh['rows'=8,'hidden'=32] {'rows'}, use_global_device_ids=true, to_apply=%region_5.6 | all-reduce | flops 262144 | bytes 1572864 | tf_op jit(solution)/shard_map/psum | solution.py:61
  279.0 1.0 dynamic-slice_convert_fusion
  280.0 0.0 copy-start.1
  280.0 5.5 fusion.12
  285.5 4.1 fusion.10
  289.6 19.9 %gather_fusion.1 = f32[1024,896]{1,0:T(8,128)} fusion(f32[64,32,896]{2,1,0:T(8,128)} %fusion.12, s32[1024]{0:T(1024)S(1)} %bitcast.78), kind=kCustom, calls=%fused_computation.1 | custom fusion | bytes 7348224 | tf_op jit(solution)/shard_map/gather | solution.py:73
  309.5 19.9 %gather_fusion.2 = f32[1024,896]{1,0:T(8,128)} fusion(f32[64,32,896]{2,1,0:T(8,128)} %fusion.10, s32[1024]{0:T(1024)S(1)} %bitcast.79), kind=kCustom, calls=%fused_computation.2 | custom fusion | bytes 7348224 | tf_op jit(solution)/shard_map/gather | solution.py:73
  329.4 7.5 %fusion = bf16[1024,2,896]{2,0,1:T(8,128)(2,1)} fusion(f32[1024,1,896]{2,0,1:T(8,128)} %convolution_bitcast_fusion, f32[1024,1,896]{2,0,1:T(8,128)} %convolution_bitcast_fusion.1, f32[1024,1,896]{2,0,1:T(8,128)} %bitcast.81, f32[1024,1,896]{2,0,1:T(8,128)} %bitcast.80), kind=kLoop, calls=%fused_computation.7 | loop fusion | flops 7340032 | bytes 18350080 | tf_op jit(solution)/shard_map/convert_element_type | solution.py:79
  336.8 0.0 all-reduce.7.cloned.1.call-update
  336.9 0.2 reduce-scatter.2.cloned.1.call-start
  337.1 0.1 copy.22
  337.2 0.1 reshape.98
  337.3 0.1 copy.21
  337.4 0.1 dynamic-slice_bitcast_fusion
  337.5 0.1 copy.20
  337.5 0.1 reshape.70
  337.6 97.2 %all-reduce.7.cloned.1.call-done = bf16[1024,2,896]{2,0,1:T(8,128)(2,1)} async-done(((bf16[1024,2,896]{2,0,1:T(8,128)(2,1)}), bf16[1024,2,896]{2,0,1:T(8,128)(2,1)}) %all-reduce.7.cloned.1.call-update) | async-done | bytes 3670032 | tf_op jit(solution)/shard_map/psum | solution.py:78
  434.8 2.5 convert_element_type.29
  437.3 2.3 fusion.3
  439.6 12.3 %gather_fusion.3 = bf16[2048,896]{1,0:T(8,128)(2,1)} fusion(bf16[1024,896]{1,0:T(8,128)(2,1)} %fusion.3, s32[2048]{0:T(1024)S(1)} %broadcast_clamp_fusion), kind=kCustom, calls=%fused_computation.3 | custom fusion | bytes 7348224 | tf_op jit(solution)/shard_map/gather | solution.py:83
  451.9 0.0 copy-done.5
  451.9 4.2 fusion.4
  456.1 0.1 broadcast_in_dim.54
  456.2 5.2 dynamic_update_slice.7
  461.3 86.1 %all-reduce.9 = bf16[64,32,64]{2,1,0:T(8,128)(2,1)S(1)} all-reduce(f32[64,32,64]{2,1,0:T(8,128)S(1)} %dynamic_update_slice.7), channel_id=1, replica_groups=mesh['rows'=8,'hidden'=32] {'rows','hidden'}, use_global_device_ids=true, to_apply=%region_7.8 | all-reduce | flops 131072 | bytes 786432 | tf_op jit(solution)/shard_map/psum | solution.py:92
  547.5 1.1 fusion.24
  548.6 3.3 scatter_custom_fusion
  551.8 6.4 fusion.1
  558.2 0.0 reduce-scatter.2.cloned.1.call-update
  558.3 85.7 %reduce-scatter.2.cloned.1.call-done = bf16[32,1024]{1,0:T(8,128)(2,1)} async-done(((bf16[1024,1024]{1,0:T(8,128)(2,1)}), bf16[32,1024]{1,0:T(8,128)(2,1)}) %reduce-scatter.2.cloned.1.call-update) | async-done | bytes 65552 | tf_op jit(solution)/shard_map/reduce_scatter | solution.py:105
  (19 shorter events, 0.1 us)
Async XLA Ops:
  6.5 545.3 %copy-start = (bf16[896,1024]{1,0:T(8,128)(2,1)S(1)}, bf16[896,1024]{1,0:T(8,128)(2,1)}, u32[]{:S(2)}) copy-start(bf16[896,1024]{1,0:T(8,128)(2,1)} %param.13) | copy-start | bytes 5505028
  6.5 57.5 %copy-start.3 = (bf16[2,1024,128]{2,1,0:T(8,128)(2,1)S(1)}, bf16[2,1024,128]{2,1,0:T(8,128)(2,1)}, u32[]{:S(2)}) copy-start(bf16[2,1024,128]{2,1,0:T(8,128)(2,1)} %param.14) | copy-start | bytes 1572868
  6.5 54.8 %all-gather.2.cloned.1.call-start = ((), (), s32[]{:S(2)}) async-start(), calls=%async_computation.1 | async-start | bytes 2162688 | tf_op jit(solution)/shard_map/all_gather | solution.py:51
  7.3 181.4 %all-reduce.5.cloned.1.call-start = ((), (), s32[]{:S(2)}) async-start(), calls=%async_computation.2 | async-start | bytes 8388608 | tf_op jit(solution)/shard_map/psum | solution.py:61
  67.7 367.1 %all-reduce.7.cloned.1.call-start = ((), (), s32[]{:S(2)}) async-start(), calls=%async_computation.3 | async-start | bytes 7340032 | tf_op jit(solution)/shard_map/psum | solution.py:78
  67.7 6.4 copy-start.2
  67.7 6.4 copy-start.4
  280.0 5.5 copy-start.1
  336.9 307.1 %reduce-scatter.2.cloned.1.call-start = ((), (), s32[]{:S(2)}) async-start(), calls=%async_computation.4 | async-start | bytes 2162688 | tf_op jit(solution)/shard_map/reduce_scatter | solution.py:105
  439.6 12.3 %copy-start.5 = (bf16[64,8,896]{2,1,0:T(8,128)(2,1)S(1)}, bf16[64,8,896]{2,1,0:T(8,128)(2,1)}, u32[]{:S(2)}) copy-start(bf16[64,8,896]{2,1,0:T(8,128)(2,1)} %param.16) | copy-start | bytes 2752516
Sparse Core Ops, SparseCore 0:
  9.9 51.3 all-gather.1
  67.8 120.8 all-reduce.4
  337.0 97.7 all-reduce.6
  558.4 85.4 reduce-scatter.1
